TPU v7x, 256 devices: a whole 4x4x8 slice. The times are simulated.
256 devices in a mesh: section: 32 (over y, z), group: 8 (over x, core).
Axes of the slice: x: 4, y: 4, z: 8, core: 2. Of those that a mesh axis runs over, the one named last changes fastest.
Arguments:
- query_rows: bfloat16 [16384, 8192], P('section', 'group'), may hold values from -6 to 6
- key_rows: bfloat16 [16384, 8192], P('section', 'group'), may hold values from -6 to 6
- value_rows: bfloat16 [16384, 8192], P('section', 'group'), may hold values from -6 to 6
- log_decay: float32 [16384, 64], P('section', 'group'), may hold values from -1 to 0
- norm_gain: float32 [8192], P('group'), may hold values from 0.1 to 1.9
- out_proj: bfloat16 [8192, 6144], P('group', 'section'), may hold values from -0.0625 to 0.0625
Outputs:
- mixed: bfloat16 [16384, 6144], P('section', 'group')
All inputs are finite; a program needn't handle non-finite values.
Results may differ from a plain program's by a relative error of at most 0.015.
Values may be sent and summed in bfloat16 or wider, within the bound.
A program may use at most 128 MiB of HBM per device.

v0:
```python
import jax
import jax.numpy as jnp
from jax import lax
from jax.sharding import PartitionSpec as P

BLOCK = 512


def carried_in(value, axis, join, neutral):
    place = lax.axis_index(axis)
    gathered = jax.tree.map(
        lambda a, kind: lax.all_gather(a.astype(kind), axis), value, (jnp.bfloat16, jnp.bfloat16)
    )
    state = jax.tree.map(lambda a, e: jnp.zeros_like(a) + jnp.asarray(e, a.dtype), value, neutral)

    def one(turn, state):
        return join(
            state,
            jax.tree.map(
                lambda a, own: lax.dynamic_index_in_dim(a, turn, 0, False).astype(own.dtype),
                gathered,
                value,
            ),
        )

    return lax.fori_loop(0, place, one, state)


def span_core(query, key, value, decay):
    cumul = jnp.cumsum(decay, axis=0)
    total = cumul[-1]
    scores = jnp.einsum("thd,shd->hts", query, key, preferred_element_type=jnp.float32)
    length = decay.shape[0]
    token_positions = jnp.arange(length)
    causal = (token_positions[:, None] >= token_positions[None, :])[None]
    spread = cumul.T[:, :, None] - cumul.T[:, None, :]
    factor = jnp.where(causal, jnp.exp(jnp.where(causal, spread, 0.0)), 0.0)
    weights = (scores * factor).astype(jnp.bfloat16)
    intra = jnp.einsum("hts,she->the", weights, value, preferred_element_type=jnp.float32)
    scaled_keys = key.astype(jnp.float32) * jnp.exp(total[None, :] - cumul)[:, :, None]
    update = jnp.einsum(
        "shd,she->hde", scaled_keys, value.astype(jnp.float32), precision=lax.Precision.HIGHEST
    )
    return (intra, cumul, total, update)


def normalize(attended, gain):
    moment = jnp.mean(attended * attended, axis=-1, keepdims=True)
    return (attended * lax.rsqrt(moment + 1e-06) * gain).astype(jnp.bfloat16)


def combine(earlier, later):
    return (earlier[0] + later[0], jnp.exp(later[0])[:, None, None] * earlier[1] + later[1])


def shards(query_rows, key_rows, value_rows, log_decay, norm_gain, out_proj):
    tokens_here, width = query_rows.shape
    heads = log_decay.shape[1]
    size = width // heads
    blocks = tokens_here // BLOCK
    query_all = query_rows.reshape(blocks, BLOCK, heads, size)
    key_all = key_rows.reshape(blocks, BLOCK, heads, size)
    value_all = value_rows.reshape(blocks, BLOCK, heads, size)
    decay_all = log_decay.reshape(blocks, BLOCK, heads)
    gain = norm_gain.reshape(heads, size)

    def local_step(carry, pieces):
        run_log, run_state = carry
        query, key, value, decay = pieces
        intra, cumul, total, update = span_core(query, key, value, decay)
        carry_next = (run_log + total, jnp.exp(total)[:, None, None] * run_state + update)
        return (carry_next, (intra, cumul, run_log, run_state))

    empty = (jnp.zeros((heads,), jnp.float32), jnp.zeros((heads, size, size), jnp.float32))
    local_total, gathered = lax.scan(local_step, empty, (query_all, key_all, value_all, decay_all))
    intra, cumul, before_log, before_state = gathered
    local_log, local_state = local_total
    prefix = carried_in((local_log, local_state), "section", combine, empty)
    incoming = prefix[1]
    states = jnp.exp(before_log)[:, :, None, None] * incoming[None] + before_state
    lifted = query_all.astype(jnp.float32) * jnp.exp(cumul)[..., None]
    inter = jnp.einsum("cthd,chde->cthe", lifted, states, precision=lax.Precision.HIGHEST)
    normed = normalize(intra + inter, gain).reshape(tokens_here, width)
    groups = lax.axis_size("group")
    full_columns = lax.all_gather(out_proj, "section", axis=1, tiled=True)
    slab = lax.all_to_all(full_columns, "group", split_axis=1, concat_axis=0, tiled=True)
    all_normed = lax.all_gather(normed, "group", axis=1, tiled=True)
    columns = slab.shape[1]
    pieces = jnp.einsum(
        "tgk,gkd->gtd",
        all_normed.reshape(tokens_here, groups, width),
        slab.reshape(groups, width, columns),
        preferred_element_type=jnp.float32,
    ).astype(jnp.bfloat16)
    return jnp.sum(pieces.astype(jnp.float32), axis=0).astype(jnp.bfloat16)


def solution(mesh):
    return jax.shard_map(
        shards,
        mesh=mesh,
        in_specs=(
            P("section", "group"),
            P("section", "group"),
            P("section", "group"),
            P("section", "group"),
            P("group"),
            P("group", "section"),
        ),
        out_specs=P("section", "group"),
        check_vma=False,
    )
```

profile of v0, /device:TPU:16, one launch (start us, length us, event | category | flops | bytes accessed | tf_op | source)
XLA Modules:
  0.0 439.9 jit_solution(82016181733458772)
XLA Ops:
  6.5 2.3 reduce-window.6
  9.4 1.5 copy.50
  10.9 3.2 fusion.19
  15.1 41.2 %all-gather.1 = bf16[32,1,8]{2,1,0:T(2,128)(2,1)S(1)} all-gather(bf16[1,1,8]{2,1,0:T(2,128)(2,1)S(1)} %bitcast.83), channel_id=1, replica_groups=mesh['section'=32,'group'=8] {'section'}, dimensions={0}, use_global_device_ids=true | all-gather | bytes 528 | tf_op jit(solution)/shard_map/all_gather | solution.py:12
  56.5 6.3 %fusion.2 = f32[8,512,128]{1,2,0:T(8,128)} fusion(f32[8,512]{1,0:T(8,128)S(1)} %add_bitcast_fusion.1, pred[512,512]{1,0:T(8,128)(4,1)S(1)} %iota_compare_fusion, bf16[512,8,128]{0,2,1:T(8,128)(2,1)S(1)} %bitcast.78, bf16[512,1024]{1,0:T(8,128)(2,1)} %param.10, bf16[512,1024]{1,0:T(8,128)(2,1)S(1)} %copy-done), kind=kOutput, calls=%fused_computation.6 | convolution fusion | flops 1084227584 | bytes 5521408 | tf_op jit(solution)/shard_map/while/body/eval_jaxpr/hts,she->the/dot_general | solution.py:39
  62.8 51.3 %all-gather.10.cloned.1.call-done = bf16[256,128,128]{2,1,0:T(8,128)(2,1)} async-done(((bf16[8,128,128]{2,1,0:T(8,128)(2,1)}), bf16[256,128,128]{2,1,0:T(8,128)(2,1)}) %all-gather.10.cloned.1.call-update) | async-done | bytes 8388624 | tf_op jit(solution)/shard_map/all_gather | solution.py:12
  114.1 18.4 %while.3 = (s32[]{:T(128)}, f32[8,128,128]{2,1,0:T(8,128)S(1)}, s32[]{:T(128)}, bf16[32,8]{1,0:T(8,128)(2,1)S(1)}, bf16[32,8,128,128]{3,2,1,0:T(8,128)(2,1)}, /*index=5*/s32[]{:T(128)}, s32[]{:T(128)}, s32[]{:T(128)}) while((s32[]{:T(128)}, f32[8,128,128]{2,1,0:T(8,128)S(1)}, s32[]{:T(128)}, bf16[32,8]{1,0:T(8,128)(2,1)S(1)}, ...), condition=%wide.region_3.4_spmd, body=%wide.region_2.3_spmd.sunk | while | flops 393229 | bytes 1310935 | solution.py:26
  114.1 1.1 convert_add_fusion.2
  115.3 1.1 convert_add_fusion.2
  116.4 1.1 convert_add_fusion.2
  117.6 1.1 convert_add_fusion.2
  118.7 1.1 convert_add_fusion.2
  119.9 1.1 convert_add_fusion.2
  126.8 1.1 convert_add_fusion.2
  128.0 1.1 convert_add_fusion.2
  131.4 1.1 convert_add_fusion.2
  132.5 4.2 multiply_reduce_fusion
  136.7 1.3 multiply_convert_fusion.2
  138.1 95.3 %all-gather.8.cloned.1.call-done = bf16[1024,6144]{0,1:T(8,128)(2,1)} async-done(((bf16[1024,192]{0,1:T(8,128)(2,1)}), bf16[1024,6144]{0,1:T(8,128)(2,1)}) %all-gather.8.cloned.1.call-update) | async-done | bytes 12582928 | tf_op jit(solution)/shard_map/all_gather | solution.py:85
  233.4 16.9 %copy.45 = bf16[1024,8,768]{2,0,1:T(8,128)(2,1)} copy(bf16[1024,8,768]{0,2,1:T(8,128)(2,1)} %bitcast.75) | data formatting | bytes 25165824 | tf_op jit(solution)/shard_map/all_to_all | solution.py:86
  250.3 5.5 %all-to-all-start = ((bf16[1024,8,768]{2,0,1:T(8,128)(2,1)}), bf16[1024,8,768]{2,0,1:T(8,128)(2,1)}, u32[]{:S(2)}, u32[]{:S(2)}) async-start(bf16[1024,8,768]{2,0,1:T(8,128)(2,1)} %copy.45), calls=%async_computation | async-start | bytes 25165824 | tf_op jit(solution)/shard_map/all_to_all | solution.py:86
  255.8 71.6 %all-gather.6.cloned.1.call-done = bf16[512,8192]{0,1:T(8,128)(2,1)} async-done(((bf16[512,1024]{0,1:T(8,128)(2,1)}), bf16[512,8192]{0,1:T(8,128)(2,1)}) %all-gather.6.cloned.1.call-update) | async-done | bytes 8388624 | tf_op jit(solution)/shard_map/all_gather | solution.py:87
  327.4 92.1 %all-to-all-done = bf16[1024,8,768]{2,0,1:T(8,128)(2,1)} async-done(((bf16[1024,8,768]{2,0,1:T(8,128)(2,1)}), bf16[1024,8,768]{2,0,1:T(8,128)(2,1)}, u32[]{:S(2)}, u32[]{:S(2)}) %all-to-all-start) | async-done | bytes 12582944 | tf_op jit(solution)/shard_map/all_to_all | solution.py:86
  419.5 13.8 %convert_reduce_fusion = bf16[512,768]{1,0:T(8,128)(2,1)} fusion(bf16[512,8,1024]{0,2,1:T(8,128)(2,1)} %bitcast.84, bf16[1024,8,768]{2,0,1:T(8,128)(2,1)} %all-to-all-done), kind=kOutput, calls=%fused_computation.5 | convolution fusion | flops 6448349184 | bytes 21757952 | tf_op jit(solution)/shard_map/tgk,gkd->gtd/dot_general | solution.py:89
  (46 shorter events, 9.7 us)
Async XLA Ops:
  6.5 49.9 %copy-start = (bf16[512,1024]{1,0:T(8,128)(2,1)S(1)}, bf16[512,1024]{1,0:T(8,128)(2,1)}, u32[]{:S(2)}) copy-start(bf16[512,1024]{1,0:T(8,128)(2,1)} %param.8) | copy-start | bytes 3145732
  6.5 107.5 %all-gather.10.cloned.1.call-start = ((), (), s32[]{:S(2)}) async-start(), calls=%async_computation.3 | async-start | bytes 8650752 | tf_op jit(solution)/shard_map/all_gather | solution.py:12
  14.1 219.3 %all-gather.8.cloned.1.call-start = ((), (), s32[]{:S(2)}) async-start(), calls=%async_computation.2 | async-start | bytes 12976128 | tf_op jit(solution)/shard_map/all_gather | solution.py:85
  14.9 312.6 %all-gather.6.cloned.1.call-start = ((), (), s32[]{:S(2)}) async-start(), calls=%async_computation.1 | async-start | bytes 9437184 | tf_op jit(solution)/shard_map/all_gather | solution.py:87
  114.1 22.7 %copy-start.1 = (f32[1024]{0:T(1024)S(1)}, f32[1024]{0:T(1024)}, u32[]{:S(2)}) copy-start(f32[1024]{0:T(1024)} %param.12) | copy-start | bytes 12292
  250.3 169.2 %all-to-all-start = ((bf16[1024,8,768]{2,0,1:T(8,128)(2,1)}), bf16[1024,8,768]{2,0,1:T(8,128)(2,1)}, u32[]{:S(2)}, u32[]{:S(2)}) async-start(bf16[1024,8,768]{2,0,1:T(8,128)(2,1)} %copy.45), calls=%async_computation | async-start | bytes 25165824 | tf_op jit(solution)/shard_map/all_to_all | solution.py:86
Sparse Core Ops, SparseCore 0:
  14.3 99.7 all-gather.9
  116.6 116.7 all-gather.7
  235.3 92.1 all-gather.5
where the time goes:
time: 443 us; the launch traced here: 440 us
  waiting for transfers between devices  311 us (70%)
  blocking collectives  41.2 us (9%)
  matrix products  27.5 us (6%)
  other arithmetic  22 us (5%)
  local copies, waits for them, and re-layouts  19 us (4%)
  between operations  13.2 us (3%)
  starting transfers between devices  5.6 us (1%)
    all_gather x1, waiting for transfers between devices, shards(): full_columns = lax.all_gather(out_proj, 'section', axis=1, tiled=True)  95.3 us
    all_to_all x1, waiting for transfers between devices, shards(): lax.all_to_all(full_columns, 'group', split_axis=1, concat_axis=0, tiled=...  92.1 us
    all_gather x1, waiting for transfers between devices, shards(): all_normed = lax.all_gather(normed, 'group', axis=1, tiled=True)  71.6 us
    all_gather x1, waiting for transfers between devices, carried_in(): lax.all_gather(a.astype(kind), axis)  51.3 us
    all_gather x1, blocking collectives, carried_in(): lax.all_gather(a.astype(kind), axis)  41.2 us
    add x16, other arithmetic, combine(): jnp.exp(later[0])[:, None, None] * earlier[1] + later[1]  17.8 us
    all_to_all x1, local copies, waits for them, and re-layouts, shards(): lax.all_to_all(full_columns, 'group', split_axis=1, concat_axis=0, tiled=...  16.9 us
    dot_general x1, matrix products, shards(): jnp.einsum('tgk,gkd->gtd', all_normed.reshape(tokens_here, groups, width)...  13.8 us
  transfers between devices with their start and end apart: 4, of which 4 were waited for; matrix products, arithmetic and copies ran while one was open for 11% of the time, Pallas kernels for 0%

commit v1 on v0

v1 whole, which is shorter than its diff:
```python
import functools

import jax
import jax.numpy as jnp
from jax import lax
from jax.experimental import pallas as pl
from jax.experimental.pallas import tpu as pltpu
from jax.sharding import PartitionSpec as P

BF = jnp.bfloat16
F32 = jnp.float32
MESH = pl.DeviceIdType.MESH
TOK = 512
HALF = 256
HEADS = 8
HD = 128
WIDTH = HEADS * HD
PIECE = 192
CUT = 96
NY, NZ, NX, NS = 4, 8, 4, 32
SLOT = 48
PART = 32
STEPS = (0, -1, 1, 2)
ROWS = (0, 1, -1, 2)


def nt(a, b):
    return lax.dot_general(a, b, (((1,), (1,)), ((), ())), preferred_element_type=F32)


def tn(a, b):
    return lax.dot_general(a, b, (((0,), (0,)), ((), ())), preferred_element_type=F32)


def nn(a, b):
    return jnp.dot(a, b, preferred_element_type=F32)


def kernel(
    q_hbm, k_hbm, v_hbm, w_hbm, decay_ref, gain_ref, out_hbm,
    qb, kb, vb, wraw, wb, ab, intra, colc, rowc, ust, urecv, pst, precv, factor,
    dbuf, fbuf, xrecv, fin, otb,
    load_sem, out_sem, wz_s, wz_r, wy_s, wy_r, st_s, st_r, a_s, a_r, d_s, d_r, x_s, x_r, b_s, b_r,
):
    sec = lax.axis_index("section")
    grp = lax.axis_index("group")
    y, z = sec // NZ, lax.rem(sec, NZ)
    x, c = grp // 2, lax.rem(grp, 2)
    h, k0 = lax.rem(z, 2), z // 2

    def at(dy, dz):
        return (lax.rem(y + dy + NY, NY) * NZ + lax.rem(z + dz + NZ, NZ), grp)

    mate = (sec, x * 2 + 1 - c)

    def along_x(xx):
        return (sec, xx * 2 + c)

    def remote(src, dst, ssem, rsem, dev):
        return pltpu.make_async_remote_copy(
            src_ref=src, dst_ref=dst, send_sem=ssem, recv_sem=rsem, device_id=dev, device_id_type=MESH
        )

    loads = [
        pltpu.make_async_copy(s, d, load_sem.at[i])
        for i, (s, d) in enumerate(((w_hbm, wraw), (k_hbm, kb), (v_hbm, vb), (q_hbm, qb)))
    ]
    for cp in loads:
        cp.start()
    bar = pltpu.get_barrier_semaphore()

    def greet(i, _):
        pl.semaphore_signal(bar, inc=1, device_id=(lax.rem(sec + i, NS), grp), device_id_type=MESH)
        return 0

    lax.fori_loop(1, NS, greet, 0)
    pl.semaphore_signal(bar, inc=1, device_id=mate, device_id_type=MESH)
    for i in range(1, NX):
        pl.semaphore_signal(bar, inc=1, device_id=along_x(lax.rem(x + i, NX)), device_id_type=MESH)

    d = jnp.concatenate([decay_ref[...], jnp.zeros((TOK, HD - HEADS), F32)], axis=1)
    hi = d.astype(BF)
    rest = d - hi.astype(F32)
    mid = rest.astype(BF)
    low = (rest - mid.astype(F32)).astype(BF)
    tri = (
        lax.broadcasted_iota(jnp.int32, (TOK, TOK), 0) >= lax.broadcasted_iota(jnp.int32, (TOK, TOK), 1)
    ).astype(F32).astype(BF)
    cum = nn(tri, hi) + (nn(tri, mid) + nn(tri, low))
    colc[...] = cum
    rowc[...] = cum.T[0:HEADS]

    loads[0].wait()
    wb[y, k0] = wraw[...].T
    pl.semaphore_wait(bar, NS - 1 + 1 + NX - 1)

    def wz(i):
        if i < 2:
            ref = wb.at[y, k0]
            dz = 2 if i == 0 else -2
        elif i == 2:
            ref = wb.at[y, lax.rem(k0 + 3, 4), pl.ds(0, CUT)]
            dz = 2
        else:
            ref = wb.at[y, lax.rem(k0 + 1, 4), pl.ds(CUT, CUT)]
            dz = -2
        return remote(ref, ref, wz_s.at[i], wz_r.at[i], at(0, dz))

    def wz_wait(i):
        if i < 2:
            ref = wb.at[y, lax.rem(k0 + (3 if i == 0 else 1), 4)]
        else:
            ref = wb.at[y, lax.rem(k0 + 2, 4), pl.ds(0 if i == 2 else CUT, CUT)]
        remote(ref, ref, wz_s.at[i], wz_r.at[i], at(0, 0)).wait_recv()

    def kq(q):
        return lax.rem(k0 + STEPS[q] + 4, 4)

    def wy(q, i):
        if i < 2:
            ref = wb.at[y, kq(q)]
            dy = 1 if i == 0 else -1
        elif i == 2:
            ref = wb.at[lax.rem(y + 3, NY), kq(q), pl.ds(0, CUT)]
            dy = 1
        else:
            ref = wb.at[lax.rem(y + 1, NY), kq(q), pl.ds(CUT, CUT)]
            dy = -1
        return remote(ref, ref, wy_s.at[q, i], wy_r.at[q, i], at(dy, 0))

    def wy_wait(q, i):
        if i < 2:
            ref = wb.at[lax.rem(y + (3 if i == 0 else 1), NY), kq(q)]
        else:
            ref = wb.at[lax.rem(y + 2, NY), kq(q), pl.ds(0 if i == 2 else CUT, CUT)]
        remote(ref, ref, wy_s.at[q, i], wy_r.at[q, i], at(0, 0)).wait_recv()

    def y_send(q):
        wy(q, 0).start()
        wy(q, 1).start()

    def y_forward(q):
        wy_wait(q, 0)
        wy(q, 2).start()
        wy_wait(q, 1)
        wy(q, 3).start()

    wz(0).start()
    wz(1).start()
    y_send(0)

    loads[1].wait()
    loads[2].wait()
    total = rowc[:, TOK - 1:TOK] + jnp.zeros((HEADS, HD), F32)
    total_hi = total.astype(BF)
    total_lo = (total - total_hi.astype(F32)).astype(BF)
    tail = jnp.concatenate([total_hi.astype(F32), total_lo.astype(F32)], axis=0).astype(BF)
    for j in range(NS):
        ust[j, PART:SLOT] = tail
    for i in range(HEADS):
        col = colc[:, i:i + 1]
        last = colc[TOK - 1:TOK, i:i + 1]
        keys = (kb[:, i * HD:(i + 1) * HD].astype(F32) * jnp.exp(last - col)).astype(BF)
        upd = tn(keys, vb[:, i * HD:(i + 1) * HD]).astype(BF)
        for j in range(4):
            ust[4 * i + j, 0:PART] = upd[j * PART:(j + 1) * PART]

    def send_update(i, _):
        to = lax.rem(sec + i, NS)
        remote(ust.at[to], urecv.at[sec], st_s.at[0], st_r.at[0], (to, grp)).start()
        return 0

    lax.fori_loop(1, NS, send_update, 0)
    urecv[sec] = ust[sec]

    loads[3].wait()
    causal = lax.broadcasted_iota(jnp.int32, (HALF, HALF), 0) >= lax.broadcasted_iota(jnp.int32, (HALF, HALF), 1)

    def inside(i):
        cols = slice(i * HD, (i + 1) * HD)
        for b in range(2):
            rows = slice(b * HALF, (b + 1) * HALF)
            qt = qb[rows, cols]
            col = colc[rows, i:i + 1]
            acc = None
            for e in range(b + 1):
                sl = slice(e * HALF, (e + 1) * HALF)
                scores = nt(qt, kb[sl, cols])
                spread = col - rowc[i:i + 1, sl]
                if e == b:
                    spread = jnp.where(causal, spread, -1e30)
                weights = (scores * jnp.exp(spread)).astype(BF)
                term = nn(weights, vb[sl, cols])
                acc = term if acc is None else acc + term
            intra[rows, cols] = acc

    for i in range(4):
        inside(i)
    y_forward(0)

    head = sec // 4
    whole = pl.ds(0, NS - 1)
    remote(ust.at[whole], urecv.at[whole], st_s.at[0], st_r.at[0], at(0, 0)).wait_recv()
    pick = lax.rem(lax.broadcasted_iota(jnp.int32, (NS, SLOT - PART, HD), 1), HEADS) == head
    logs = jnp.sum(jnp.where(pick, urecv[:, PART:SLOT, :].astype(F32), 0.0), axis=1)
    factor[...] = jnp.exp(logs)
    state = jnp.zeros((PART, HD), F32)
    for j in range(NS):
        pst[j] = state.astype(BF)
        if j < NS - 1:
            state = state * factor[j:j + 1, :] + urecv[j, 0:PART, :].astype(F32)

    def send_state(i, _):
        to = lax.rem(sec + i, NS)
        remote(pst.at[to], precv.at[sec], st_s.at[1], st_r.at[1], (to, grp)).start()
        return 0

    lax.fori_loop(1, NS, send_state, 0)
    precv[sec] = pst[sec]

    for i in range(4, HEADS):
        inside(i)
    wz_wait(0)
    wz(2).start()
    wz_wait(1)
    wz(3).start()
    y_send(1)
    y_send(2)

    remote(pst.at[whole], precv.at[whole], st_s.at[1], st_r.at[1], at(0, 0)).wait_recv()

    def a_send(i):
        src = ab.at[pl.ds(i * HALF, HALF)]
        dst = ab.at[pl.ds(TOK + i * HALF, HALF)]
        return remote(src, dst, a_s.at[i], a_r.at[i], at(0, -1 if i == 0 else 1))

    for i in range(HEADS):
        cols = slice(i * HD, (i + 1) * HD)
        carried = precv[4 * i:4 * i + 4].reshape(HD, HD)
        att = intra[:, cols] + jnp.exp(colc[:, i:i + 1]) * nn(qb[:, cols], carried)
        moment = jnp.mean(att * att, axis=1, keepdims=True)
        ab[0:TOK, cols] = (att * lax.rsqrt(moment + 1e-6) * gain_ref[i:i + 1, :]).astype(BF)
    a_send(0).start()
    a_send(1).start()

    def names(q, r):
        yy = lax.rem(y + ROWS[r] + NY, NY)
        k = kq(q)
        return yy, k, (k // 2) == c, lax.rem(k, 2)

    def mate_copy(n):
        return remote(dbuf.at[n], dbuf.at[n], d_s.at[n], d_r.at[n], mate)

    def x_copy(n, yy, kk, half):
        return remote(dbuf.at[n], xrecv.at[x, kk, half], x_s.at[n], x_r.at[x, kk, half], along_x(yy))

    def compute(n, unit):
        q, r, half = unit
        yy, k, mine, kk = names(q, r)
        res = nt(wb[yy, k], ab[half * TOK:(half + 1) * TOK])

        @pl.when(mine)
        def _():
            fbuf[n % 2] = res

        @pl.when(jnp.logical_not(mine))
        def _():
            dbuf[n] = res.astype(BF)
            mate_copy(n).start()

    def finish(n, unit):
        q, r, half = unit
        yy, k, mine, kk = names(q, r)

        @pl.when(mine)
        def _():
            mate_copy(n).wait_recv()
            val = (fbuf[n % 2] + dbuf[n].astype(F32)).astype(BF)

            @pl.when(yy == x)
            def _():
                xrecv[x, kk, half] = val

            @pl.when(yy != x)
            def _():
                dbuf[n] = val
                x_copy(n, yy, kk, half).start()

    order = []

    def add(q, rows, half):
        order.extend([(q, r, half) for r in rows])

    hooks = {}

    def hook(fn):
        hooks.setdefault(len(order), []).append(fn)

    def z_last():
        wz_wait(2)
        wz_wait(3)
        y_send(3)

    def a_wait():
        for i in range(2):
            a_send(i).wait_recv()

    add(0, (0, 1, 2), 0)
    hook(lambda: (wy_wait(0, 2), wy_wait(0, 3)))
    add(0, (3,), 0)
    add(1, (0,), 0)
    add(2, (0,), 0)
    hook(z_last)
    hook(lambda: y_forward(1))
    add(1, (1, 2), 0)
    hook(a_wait)
    add(0, (0, 1, 2, 3), 1)
    hook(lambda: y_forward(2))
    add(1, (0, 1, 2), 1)
    hook(lambda: (wy_wait(1, 2), wy_wait(1, 3)))
    add(1, (3,), 0)
    add(1, (3,), 1)
    add(2, (1, 2), 0)
    add(2, (0, 1, 2), 1)
    add(3, (0,), 0)
    add(3, (0,), 1)
    hook(lambda: (wy_wait(2, 2), wy_wait(2, 3)))
    add(2, (3,), 0)
    add(2, (3,), 1)
    hook(lambda: y_forward(3))
    add(3, (1, 2), 0)
    add(3, (1, 2), 1)
    hook(lambda: (wy_wait(3, 2), wy_wait(3, 3)))
    add(3, (3,), 0)
    add(3, (3,), 1)

    for n, unit in enumerate(order):
        for fn in hooks.get(n, ()):
            fn()
        compute(n, unit)
        if n:
            finish(n - 1, order[n - 1])
    finish(len(order) - 1, order[-1])

    def back(kk, i):
        src = fin.at[kk, :, pl.ds(i * HALF, HALF)]
        dst = otb.at[2 * kk + h, :, pl.ds(i * HALF, HALF)]
        return remote(src, dst, b_s.at[kk, i], b_r.at[kk, i], at(0, 1 if i == 0 else -1))

    def back_wait(kk, i):
        ref = otb.at[2 * kk + 1 - h, :, pl.ds(i * HALF, HALF)]
        remote(ref, ref, b_s.at[kk, i], b_r.at[kk, i], at(0, 0)).wait_recv()

    def total_of(kk, half):
        for i in range(1, NX):
            xs = lax.rem(x + i, NX)
            remote(dbuf.at[0], xrecv.at[xs, kk, half], x_s.at[0], x_r.at[xs, kk, half], mate).wait_recv()
        acc = xrecv[0, kk, half].astype(F32) + xrecv[1, kk, half].astype(F32)
        acc = acc + (xrecv[2, kk, half].astype(F32) + xrecv[3, kk, half].astype(F32))
        return acc.astype(BF)

    for kk in range(2):
        fin[kk] = total_of(kk, 1)
        back(kk, 0).start()
        back(kk, 1).start()
    for kk in range(2):
        otb[2 * kk + h] = total_of(kk, 0)
    for kk in range(2):
        for i in range(2):
            back_wait(kk, i)
    final = pltpu.make_async_copy(otb, out_hbm, out_sem.at[0])
    final.start()

    for i in range(4):
        wz(i).wait_send()
    for q in range(4):
        for i in range(4):
            wy(q, i).wait_send()
    for i in range(2):
        a_send(i).wait_send()
    remote(ust.at[whole], urecv.at[whole], st_s.at[0], st_r.at[0], at(0, 0)).wait_send()
    remote(pst.at[whole], precv.at[whole], st_s.at[1], st_r.at[1], at(0, 0)).wait_send()
    for n, (q, r, half) in enumerate(order):
        yy, k, mine, kk = names(q, r)

        @pl.when(jnp.logical_and(mine, yy != x))
        def _():
            x_copy(n, yy, kk, half).wait_send()

        @pl.when(jnp.logical_not(mine))
        def _():
            mate_copy(n).wait_send()

    for kk in range(2):
        for i in range(2):
            back(kk, i).wait_send()
    final.wait()


def shards(query_rows, key_rows, value_rows, log_decay, norm_gain, out_proj):
    vmem = pltpu.VMEM
    dma = pltpu.SemaphoreType.DMA
    anywhere = pl.BlockSpec(memory_space=pl.ANY)
    near = pl.BlockSpec(memory_space=pltpu.VMEM)
    out = pl.pallas_call(
        kernel,
        name="parity_attention",
        out_shape=jax.ShapeDtypeStruct((4, PIECE, TOK), BF),
        in_specs=[anywhere] * 4 + [near] * 2,
        out_specs=anywhere,
        scratch_shapes=[
            vmem((TOK, WIDTH), BF),
            vmem((TOK, WIDTH), BF),
            vmem((TOK, WIDTH), BF),
            vmem((WIDTH, PIECE), BF),
            vmem((NY, 4, PIECE, WIDTH), BF),
            vmem((2 * TOK, WIDTH), BF),
            vmem((TOK, WIDTH), F32),
            vmem((TOK, HD), F32),
            vmem((HEADS, TOK), F32),
            vmem((NS, SLOT, HD), BF),
            vmem((NS, SLOT, HD), BF),
            vmem((NS, PART, HD), BF),
            vmem((NS, PART, HD), BF),
            vmem((NS, HD), F32),
            vmem((32, PIECE, TOK), BF),
            vmem((2, PIECE, TOK), F32),
            vmem((NX, 2, 2, PIECE, TOK), BF),
            vmem((2, PIECE, TOK), BF),
            vmem((4, PIECE, TOK), BF),
            dma((4,)),
            dma((1,)),
            dma((4,)),
            dma((4,)),
            dma((4, 4)),
            dma((4, 4)),
            dma((2,)),
            dma((2,)),
            dma((2,)),
            dma((2,)),
            dma((32,)),
            dma((32,)),
            dma((32,)),
            dma((NX, 2, 2)),
            dma((2, 2)),
            dma((2, 2)),
        ],
        compiler_params=pltpu.CompilerParams(
            collective_id=0, has_side_effects=True, vmem_limit_bytes=56 * 2**20
        ),
        cost_estimate=pl.CostEstimate(flops=8 * 10**9, bytes_accessed=5 * 2**20, transcendentals=2 * 10**6),
    )(query_rows, key_rows, value_rows, out_proj, log_decay, norm_gain.reshape(HEADS, HD))
    return out.reshape(4 * PIECE, TOK).T


def solution(mesh):
    return jax.shard_map(
        shards,
        mesh=mesh,
        in_specs=(
            P("section", "group"),
            P("section", "group"),
            P("section", "group"),
            P("section", "group"),
            P("group"),
            P("group", "section"),
        ),
        out_specs=P("section", "group"),
        check_vma=False,
    )
```

time: 443 us -> 118 us (0.27)
  waiting for transfers between devices: 311 us -> 0 us
  Pallas kernels: 0 us -> 112 us
  blocking collectives: 41.2 us -> 0 us
  matrix products: 27.5 us -> 0 us
  other arithmetic: 22 us -> 0 us
  between operations: 13.2 us -> 0.01 us
  local copies, waits for them, and re-layouts: 19 us -> 5.84 us
  starting transfers between devices: 5.6 us -> 0 us
    all_gather x3 -> x0, waiting for transfers between devices: 218 us -> none  [the longest x1 95.3 us: shards(): full_columns = lax.all_gather(out_proj, 'section', axis=1, tiled=True)]
    pallas_call x0 -> x1, Pallas kernels: none -> 112 us  [shards(): pl.pallas_call(kernel, name='parity_attention', out_shape=jax.ShapeDtypeS...]
    all_to_all x1 -> x0, waiting for transfers between devices: 92.1 us -> none  [shards(): lax.all_to_all(full_columns, 'group', split_axis=1, concat_axis=0, tiled=...]
    all_gather x1 -> x0, blocking collectives: 41.2 us -> none  [carried_in(): lax.all_gather(a.astype(kind), axis)]
    dot_general x4 -> x0, matrix products: 27.5 us -> none  [the longest x1 13.8 us: shards(): jnp.einsum('tgk,gkd->gtd', all_normed.reshape(tokens_here, groups, width)...]
    add x16 -> x0, other arithmetic: 17.8 us -> none  [combine(): jnp.exp(later[0])[:, None, None] * earlier[1] + later[1]]
    all_to_all x1 -> x0, local copies, waits for them, and re-layouts: 16.9 us -> none  [shards(): lax.all_to_all(full_columns, 'group', split_axis=1, concat_axis=0, tiled=...]
    all_to_all x1 -> x0, starting transfers between devices: 5.52 us -> none  [shards(): lax.all_to_all(full_columns, 'group', split_axis=1, concat_axis=0, tiled=...]
  transfers between devices with their start and end apart: 4 -> 0, of which waited for: 4 -> 0; matrix products, arithmetic and copies ran while one was open for 11% -> 0% of each run, Pallas kernels for 0% -> 0%
where the time goes in v1:
time: 118 us
  Pallas kernels  112 us (95%)
  local copies, waits for them, and re-layouts  5.84 us (5%)
    pallas_call x1, Pallas kernels, shards(): pl.pallas_call(kernel, name='parity_attention', out_shape=jax.ShapeDtypeS...  112 us
    unnamed x2, local copies, waits for them, and re-layouts  3.55 us

profile of v1, /device:TPU:16, one launch (start us, length us, event | category | flops | bytes accessed | tf_op | source)
XLA Modules:
  0.0 117.6 jit_solution(10902252201550596077)
XLA Ops:
  0.0 1.6 %copy.8.decay_ref = f32[512,8]{1,0:T(8,128)} copy(f32[512,8]{0,1:T(8,128)} %param.9) | data formatting | bytes 32768 | tf_op args[3]
  1.6 2.0 %copy.7.w_hbm = bf16[1024,192]{1,0:T(8,128)(2,1)} copy(bf16[1024,192]{0,1:T(8,128)(2,1)} %param.11) | data formatting | bytes 786432 | tf_op args[5]
  3.6 111.8 %parity_attention.1 = bf16[4,192,512]{2,1,0:T(8,128)(2,1)} custom-call(bf16[512,1024]{1,0:T(8,128)(2,1)} %q_hbm.1, bf16[512,1024]{1,0:T(8,128)(2,1)} %k_hbm.1, bf16[512,1024]{1,0:T(8,128)(2,1)} %v_hbm.1, bf16[1024,192]{1,0:T(8,128)(2,1)} %copy.7.w_hbm, f32[512,8]{1,0:T(8,128)} %copy.8.decay_ref, f32[8,128]{1,0:T(8,128)} %bitcast.4), custom_call_target="tpu_custom_call" | custom-call | flops 8000000000 | bytes 5242880 | tf_op jit(solution)/shard_map/parity_attention/pallas_call | solution.py:405
  115.3 2.3 %copy.9 = bf16[768,512]{0,1:T(8,128)(2,1)} copy(bf16[768,512]{1,0:T(8,128)(2,1)} %bitcast.3) | data formatting | bytes 1572864 | tf_op jit(solution)/shard_map/reshape | solution.py:453

commit v2 on v0

v2 whole, which is shorter than its diff:
```python
import functools

import jax
import jax.numpy as jnp
from jax import lax
from jax.experimental import pallas as pl
from jax.experimental.pallas import tpu as pltpu
from jax.sharding import PartitionSpec as P

BF = jnp.bfloat16
F32 = jnp.float32
MESH = pl.DeviceIdType.MESH
TOK = 512
HALF = 256
HEADS = 8
HD = 128
WIDTH = HEADS * HD
PIECE = 192
CUT = 96
CHUNK = 48
CHUNKS = (0, 2, 1, 3)
NY, NZ, NX = 4, 8, 4
SLOT = HD + 16


def nt(a, b):
    return lax.dot_general(a, b, (((1,), (1,)), ((), ())), preferred_element_type=F32)


def tn(a, b):
    return lax.dot_general(a, b, (((0,), (0,)), ((), ())), preferred_element_type=F32)


def nn(a, b):
    return jnp.dot(a, b, preferred_element_type=F32)


EARLY = {0: (0, 2), 7: (1, 3)}


def fold(i):
    return i + i // 2 - 2 * (i // 3)


def kernel(
    q_hbm, k_hbm, v_hbm, w_hbm, decay_ref, gain_ref, out_hbm,
    qb, kb, vb, wb, ab, intra, colc, rowc, ust, urecv, lst, lead, rst, rrecv, pst, precv,
    dbuf, fbuf, relay, own, xrecv, fin, otb,
    load_sem, out_sem, wz_s, wz_r, wy_s, wy_r, st_s, st_r, row_s, row_r, a_s, a_r, d_s, d_r, x_s, x_r, r_r, b_s, b_r,
):
    sec = lax.axis_index("section")
    grp = lax.axis_index("group")
    y, z = sec // NZ, lax.rem(sec, NZ)
    x, c = grp // 2, lax.rem(grp, 2)
    h, k0 = lax.rem(z, 2), z // 2

    def at(dy, dz):
        return (lax.rem(y + dy + NY, NY) * NZ + lax.rem(z + dz + NZ, NZ), grp)

    mate = (sec, x * 2 + 1 - c)

    def along_x(xx):
        return (sec, xx * 2 + c)

    def remote(src, dst, ssem, rsem, dev):
        return pltpu.make_async_remote_copy(
            src_ref=src, dst_ref=dst, send_sem=ssem, recv_sem=rsem, device_id=dev, device_id_type=MESH
        )

    loads = [
        pltpu.make_async_copy(s, d, load_sem.at[i])
        for i, (s, d) in enumerate(((w_hbm, wb.at[y, k0]), (k_hbm, kb), (v_hbm, vb), (q_hbm, qb)))
    ]
    for cp in loads:
        cp.start()
    bar = pltpu.get_barrier_semaphore()
    peers = [at(0, i) for i in range(1, NZ)] + [at(i, 0) for i in range(1, NY)]
    peers += [along_x(lax.rem(x + i, NX)) for i in (1, 3)] + [mate]
    for dev in peers:
        pl.semaphore_signal(bar, inc=1, device_id=dev, device_id_type=MESH)

    d = decay_ref[...]
    hi = d.astype(BF).astype(F32)
    mid = (d - hi).astype(BF).astype(F32)
    low = d - hi - mid
    tri = (
        lax.broadcasted_iota(jnp.int32, (TOK, TOK), 0) <= lax.broadcasted_iota(jnp.int32, (TOK, TOK), 1)
    ).astype(F32).astype(BF)
    cum = nn(jnp.concatenate([hi, mid, low, jnp.zeros_like(d)], axis=0).astype(BF), tri)
    cum = cum[0:HEADS] + (cum[HEADS:2 * HEADS] + cum[2 * HEADS:3 * HEADS])
    rowc[...] = cum
    colc[...] = jnp.concatenate([cum, jnp.zeros((HD - HEADS, TOK), F32)], axis=0).T

    def two_terms(val):
        top = val.astype(BF).astype(F32)
        return jnp.concatenate([top, val - top], axis=0).astype(BF)

    loads[1].wait()
    loads[2].wait()
    tail = two_terms(cum[:, TOK - 1:TOK] + jnp.zeros((HEADS, HD), F32))
    for i in range(HEADS):
        col = colc[:, i:i + 1]
        last = colc[TOK - 1:TOK, i:i + 1]
        keys = (kb[:, i * HD:(i + 1) * HD].astype(F32) * jnp.exp(last - col)).astype(BF)
        ust[i, 0:HD] = tn(keys, vb[:, i * HD:(i + 1) * HD]).astype(BF)
        ust[i, HD:SLOT] = tail
    loads[0].wait()
    pl.semaphore_wait(bar, len(peers))

    def send_z(src, dst, i):
        def one(o, _):
            to = lax.rem(z + o, NZ)
            remote(src.at[to], dst.at[z], st_s.at[i], st_r.at[i], (y * NZ + to, grp)).start()
            return 0

        lax.fori_loop(1, NZ, one, 0)

    def sent_z(src, dst, i):
        some = pl.ds(0, NZ - 1)
        return remote(src.at[some], dst.at[some], st_s.at[i], st_r.at[i], at(0, 0))

    send_z(ust, urecv, 0)

    def cut(b):
        return pl.ds(b * CUT, CUT)

    def chunk(b):
        return pl.ds(b * CHUNK, CHUNK)

    def kq(q):
        turn = 1 + 2 * lax.rem(k0, 2)
        return lax.rem(k0 + (0, turn, 4 - turn, 2)[q], 4)

    def wz(b, i):
        if i < 2:
            ref = wb.at[y, k0, chunk(b)]
            dz = 2 if i == 0 else -2
        else:
            ref = wb.at[y, lax.rem(k0 + (3 if b < 2 else 1), 4), chunk(b)]
            dz = 2 if b < 2 else -2
        return remote(ref, ref, wz_s.at[b, i], wz_r.at[b, i], at(0, dz))

    def wz_wait(b, i):
        ref = wb.at[y, lax.rem(k0 + (3, 1, 2)[i], 4), chunk(b)]
        remote(ref, ref, wz_s.at[b, i], wz_r.at[b, i], at(0, 0)).wait_recv()

    def wy(q, b, i):
        if i < 2:
            ref = wb.at[y, kq(q), chunk(b)]
            dy = 1 if i == 0 else -1
        else:
            ref = wb.at[lax.rem(y + (3 if b < 2 else 1), NY), kq(q), chunk(b)]
            dy = 1 if b < 2 else -1
        return remote(ref, ref, wy_s.at[q, b, i], wy_r.at[q, b, i], at(dy, 0))

    def wy_wait(q, b, i):
        ref = wb.at[lax.rem(y + (3, 1, 2)[i], NY), kq(q), chunk(b)]
        remote(ref, ref, wy_s.at[q, b, i], wy_r.at[q, b, i], at(0, 0)).wait_recv()

    def y_send(q, b):
        wy(q, b, 0).start()
        wy(q, b, 1).start()

    def y_forward(q, b):
        wy_wait(q, b, b // 2)
        wy(q, b, 2).start()
        wy_wait(q, b, 1 - b // 2)

    def turn(q, bs):
        for b in bs:
            y_forward(q, b)
            if q < 3:
                if q == 2:
                    wz_wait(b, 2)
                y_send(q + 1, b)

    def y_last(q):
        for b in CHUNKS:
            wy_wait(q, b, 2)

    def z_forward(b):
        wz_wait(b, b // 2)
        wz(b, 2).start()
        wz_wait(b, 1 - b // 2)
        y_send(1, b)

    for b in CHUNKS:
        y_send(0, b)

    loads[3].wait()
    causal = lax.broadcasted_iota(jnp.int32, (HALF, HALF), 0) >= lax.broadcasted_iota(jnp.int32, (HALF, HALF), 1)

    def inside(i):
        cols = slice(i * HD, (i + 1) * HD)
        for b in range(2):
            rows = slice(b * HALF, (b + 1) * HALF)
            qt = qb[rows, cols]
            col = colc[rows, i:i + 1]
            acc = None
            for e in range(b + 1):
                sl = slice(e * HALF, (e + 1) * HALF)
                scores = nt(qt, kb[sl, cols])
                spread = col - rowc[i:i + 1, sl]
                if e == b:
                    spread = jnp.where(causal, spread, -1e30)
                weights = (scores * jnp.exp(spread)).astype(BF)
                term = nn(weights, vb[sl, cols])
                acc = term if acc is None else acc + term
            intra[rows, cols] = acc

    for i in range(HEADS):
        inside(i)
        if i in EARLY:
            for b in EARLY[i]:
                wz(b, 0).start()
                wz(b, 1).start()

    urecv[z] = ust[z]
    for b in CHUNKS:
        y_forward(0, b)
    sent_z(ust, urecv, 0).wait_recv()
    pick = lax.rem(lax.broadcasted_iota(jnp.int32, (NZ, SLOT - HD, HD), 1), HEADS) == z
    logs = jnp.sum(jnp.where(pick, urecv[:, HD:SLOT, :].astype(F32), 0.0), axis=1)
    state = jnp.zeros((HD, HD), F32)
    run = jnp.zeros((1, HD), F32)
    for j in range(NZ):
        lst[j] = state
        lead[j:j + 1] = run
        state = state * jnp.exp(logs[j:j + 1]) + urecv[j, 0:HD].astype(F32)
        run = run + logs[j:j + 1]
    rst[0:HD] = state.astype(BF)
    rst[HD:SLOT] = two_terms(run + jnp.zeros((HEADS, HD), F32))

    def row_copy(i):
        return remote(rst, rrecv.at[y], row_s.at[i - 1], row_r.at[y], at(i, 0))

    for i in range(1, NY):
        row_copy(i).start()
    z_forward(0)
    z_forward(2)
    for i in range(1, NY):
        ys = lax.rem(y + i, NY)
        remote(rst, rrecv.at[ys], row_s.at[0], row_r.at[ys], at(0, 0)).wait_recv()
    state = jnp.zeros((HD, HD), F32)
    for j in range(NY - 1):
        logs = rrecv[j, HD:HD + 1].astype(F32) + rrecv[j, HD + HEADS:HD + HEADS + 1].astype(F32)
        state = jnp.where(j < y, state * jnp.exp(logs) + rrecv[j, 0:HD].astype(F32), state)
    for j in range(NZ):
        pst[j] = (lst[j] + jnp.exp(lead[j:j + 1]) * state).astype(BF)
    send_z(pst, precv, 1)
    precv[z] = pst[z]
    z_forward(1)
    z_forward(3)
    turn(1, (0, 2))
    sent_z(pst, precv, 1).wait_recv()

    def a_send(i):
        src = ab.at[pl.ds(i * HALF, HALF)]
        dst = ab.at[pl.ds(TOK + i * HALF, HALF)]
        return remote(src, dst, a_s.at[i], a_r.at[i], at(0, -1 if i == 0 else 1))

    for i in range(HEADS):
        cols = slice(i * HD, (i + 1) * HD)
        att = intra[:, cols] + jnp.exp(colc[:, i:i + 1]) * nn(qb[:, cols], precv[i])
        moment = jnp.mean(att * att, axis=1, keepdims=True)
        ab[0:TOK, cols] = (att * lax.rsqrt(moment + 1e-6) * gain_ref[i:i + 1, :]).astype(BF)
    a_send(0).start()
    a_send(1).start()
    turn(1, (1, 3))

    def names(unit):
        qs, r, half = unit
        yy = lax.rem(y + fold(r), NY)
        k = kq(qs[0])
        if len(qs) == 2:
            k = k // 2 * 2
        far = lax.rem(x + NX - yy, NX)
        return yy, half, pl.ds(k, len(qs)), (k // 2) == c, pl.ds(lax.rem(k, 2), len(qs)), far

    def mate_copy(n, unit):
        yy, half, ks, mine, kk, far = names(unit)
        ref = dbuf.at[yy, half, ks]
        return remote(ref, ref, d_s.at[n], d_r.at[n], mate)

    def relay_copy(n, unit, b):
        yy, half, ks, mine, kk, far = names(unit)
        to = along_x(lax.rem(x + (1 if b == 0 else NX - 1), NX))
        return remote(dbuf.at[yy, half, ks, cut(b)], relay.at[half, yy, ks], x_s.at[n, b], r_r.at[n], to)

    def x_copy(n, unit, g, b):
        yy, half, ks, mine, kk, far = names(unit)
        part = pl.ds(pl.multiple_of(b * CUT, CUT), CUT)
        src = dbuf.at[yy, half, ks, part]
        dst = xrecv.at[g, half, kk, part]
        return remote(src, dst, x_s.at[n, b], x_r.at[n, g, b], along_x(yy))

    def compute(n, unit):
        yy, half, ks, mine, kk, far = names(unit)
        m = len(unit[0])
        res = nt(wb[yy, ks].reshape(m * PIECE, WIDTH), ab[half * TOK:(half + 1) * TOK]).reshape(m, PIECE, TOK)

        @pl.when(mine)
        def _():
            fbuf[n % 4, 0:m] = res

        @pl.when(jnp.logical_not(mine))
        def _():
            dbuf[yy, half, ks] = res.astype(BF)
            mate_copy(n, unit).start()

    def pair(n, unit):
        yy, half, ks, mine, kk, far = names(unit)
        m = len(unit[0])

        @pl.when(mine)
        def _():
            mate_copy(n, unit).wait_recv()
            val = (fbuf[n % 4, 0:m] + dbuf[yy, half, ks].astype(F32)).astype(BF)

            @pl.when(far == 0)
            def _():
                own[half, kk] = val

            @pl.when(far != 0)
            def _():
                dbuf[yy, half, ks] = val

            @pl.when(far == 2)
            def _():
                relay_copy(n, unit, 0).start()
                relay_copy(n, unit, 1).start()

            @pl.when(far == 1)
            def _():
                x_copy(n, unit, 1, 0).start()

            @pl.when(far == 3)
            def _():
                x_copy(n, unit, 0, 1).start()

    def passed(n, unit):
        yy, half, ks, mine, kk, far = names(unit)

        @pl.when(jnp.logical_and(mine, lax.rem(far, 2) == 1))
        def _():
            g = 1 - far // 2
            part = pl.ds(pl.multiple_of(g * CUT, CUT), CUT)
            came = relay.at[half, yy, ks]
            remote(came, came, x_s.at[n, 0], r_r.at[n], mate).wait_recv()
            dbuf[yy, half, ks, part] = (dbuf[yy, half, ks, part].astype(F32) + came[...].astype(F32)).astype(BF)
            x_copy(n, unit, g, g).start()

    def back(kk, i):
        src = fin.at[kk, :, pl.ds(i * HALF, HALF)]
        dst = otb.at[2 * kk + h, :, pl.ds(i * HALF, HALF)]
        return remote(src, dst, b_s.at[kk, i], b_r.at[kk, i], at(0, 1 if i == 0 else -1))

    def back_wait(kk, i):
        ref = otb.at[2 * kk + 1 - h, :, pl.ds(i * HALF, HALF)]
        remote(ref, ref, b_s.at[kk, i], b_r.at[kk, i], at(0, 0)).wait_recv()

    def total(n, unit):
        yy, half, ks, mine, kk, far = names(unit)
        m = len(unit[0])

        @pl.when(jnp.logical_and(mine, far == 0))
        def _():
            for g in range(2):
                for b in range(2):
                    ref = xrecv.at[g, half, kk, cut(b)]
                    remote(ref, ref, x_s.at[n, 0], x_r.at[n, g, b], mate).wait_recv()
            for j in range(m):
                one = j if m == 2 else lax.rem(kq(unit[0][0]), 2)
                acc = xrecv[0, half, one].astype(F32) + xrecv[1, half, one].astype(F32)
                acc = (acc + own[half, one].astype(F32)).astype(BF)
                if half == 0:
                    otb[2 * one + h] = acc
                else:
                    fin[one] = acc
                    back(one, 0).start()
                    back(one, 1).start()

    order = []
    hooks = {}

    def add(qs, rows, halves):
        for r in rows:
            order.extend([(qs, r, half) for half in halves])

    def hook(fn):
        hooks.setdefault(len(order), []).append(fn)

    def a_wait():
        for i in range(2):
            a_send(i).wait_recv()

    add((0,), (0, 1, 2), (0,))
    hook(lambda: y_last(0))
    add((0,), (3,), (0,))
    add((1,), (0, 1, 2), (0,))
    hook(lambda: turn(2, (0, 2)))
    hook(lambda: y_last(1))
    add((1,), (3,), (0,))
    hook(lambda: turn(2, (1, 3)))
    add((2,), (0, 1, 2), (0,))
    hook(a_wait)
    add((0, 1), (0, 1), (1,))
    hook(lambda: turn(3, (0, 2)))
    add((0, 1), (2, 3), (1,))
    add((2,), (0, 1, 2), (1,))
    hook(lambda: y_last(2))
    add((2,), (3,), (1, 0))
    add((3,), (0,), (1, 0))
    hook(lambda: turn(3, (1, 3)))
    add((3,), (1, 2), (1, 0))
    hook(lambda: y_last(3))
    add((3,), (3,), (1, 0))

    stages = ((0, compute), (3, pair), (9, passed), (20, total))
    for n in range(len(order) + stages[-1][0]):
        for fn in hooks.get(n, ()):
            fn()
        for lag, fn in stages:
            if 0 <= n - lag < len(order):
                fn(n - lag, order[n - lag])

    for kk in range(2):
        for i in range(2):
            back_wait(kk, i)
    final = pltpu.make_async_copy(otb, out_hbm, out_sem.at[0])
    final.start()

    for b in CHUNKS:
        for i in range(3):
            wz(b, i).wait_send()
            for q in range(4):
                wy(q, b, i).wait_send()
    for i in range(2):
        a_send(i).wait_send()
    sent_z(ust, urecv, 0).wait_send()
    sent_z(pst, precv, 1).wait_send()
    for i in range(1, NY):
        row_copy(i).wait_send()
    for n, unit in enumerate(order):
        yy, half, ks, mine, kk, far = names(unit)

        @pl.when(jnp.logical_and(mine, far != 0))
        def _():
            relay_copy(n, unit, 0).wait_send()
            relay_copy(n, unit, 1).wait_send()

        @pl.when(jnp.logical_not(mine))
        def _():
            mate_copy(n, unit).wait_send()

        @pl.when(jnp.logical_and(jnp.logical_and(mine, far == 0), half == 1))
        def _():
            for j in range(len(unit[0])):
                one = j if len(unit[0]) == 2 else lax.rem(kq(unit[0][0]), 2)
                back(one, 0).wait_send()
                back(one, 1).wait_send()

    final.wait()


def shards(query_rows, key_rows, value_rows, log_decay, norm_gain, out_proj):
    vmem = pltpu.VMEM
    dma = pltpu.SemaphoreType.DMA
    anywhere = pl.BlockSpec(memory_space=pl.ANY)
    near = pl.BlockSpec(memory_space=pltpu.VMEM)
    out = pl.pallas_call(
        kernel,
        name="parity_attention",
        out_shape=jax.ShapeDtypeStruct((4, PIECE, TOK), BF),
        in_specs=[anywhere] * 4 + [near] * 2,
        out_specs=anywhere,
        scratch_shapes=[
            vmem((TOK, WIDTH), BF),
            vmem((TOK, WIDTH), BF),
            vmem((TOK, WIDTH), BF),
            vmem((NY, 4, PIECE, WIDTH), BF),
            vmem((2 * TOK, WIDTH), BF),
            vmem((TOK, WIDTH), F32),
            vmem((TOK, HD), F32),
            vmem((HEADS, TOK), F32),
            vmem((NZ, SLOT, HD), BF),
            vmem((NZ, SLOT, HD), BF),
            vmem((NZ, HD, HD), F32),
            vmem((NZ, HD), F32),
            vmem((SLOT, HD), BF),
            vmem((NY, SLOT, HD), BF),
            vmem((NZ, HD, HD), BF),
            vmem((NZ, HD, HD), BF),
            vmem((NY, 2, 4, PIECE, TOK), BF),
            vmem((4, 2, PIECE, TOK), F32),
            vmem((2, NY, 4, CUT, TOK), BF),
            vmem((2, 2, PIECE, TOK), BF),
            vmem((2, 2, 2, PIECE, TOK), BF),
            vmem((2, PIECE, TOK), BF),
            vmem((4, PIECE, TOK), BF),
            dma((4,)),
            dma((1,)),
            dma((4, 3)),
            dma((4, 3)),
            dma((4, 4, 3)),
            dma((4, 4, 3)),
            dma((2,)),
            dma((2,)),
            dma((NY - 1,)),
            dma((NY,)),
            dma((2,)),
            dma((2,)),
            dma((32,)),
            dma((32,)),
            dma((32, 2)),
            dma((32, 2, 2)),
            dma((32,)),
            dma((2, 2)),
            dma((2, 2)),
        ],
        compiler_params=pltpu.CompilerParams(
            collective_id=0, has_side_effects=True, vmem_limit_bytes=56 * 2**20
        ),
        cost_estimate=pl.CostEstimate(flops=8 * 10**9, bytes_accessed=5 * 2**20, transcendentals=2 * 10**6),
    )(query_rows, key_rows, value_rows, out_proj.T, log_decay.T, norm_gain.reshape(HEADS, HD))
    return out.reshape(4 * PIECE, TOK).T


def solution(mesh):
    return jax.shard_map(
        shards,
        mesh=mesh,
        in_specs=(
            P("section", "group"),
            P("section", "group"),
            P("section", "group"),
            P("section", "group"),
            P("group"),
            P("group", "section"),
        ),
        out_specs=P("section", "group"),
        check_vma=False,
    )
```

time: 443 us -> 99.9 us (0.23)
  the two profiles are of different devices: /device:TPU:16 before, /device:TPU:37 now
where the time goes in v2:
time: 99.9 us; the launch traced here: 99.6 us
  Pallas kernels  97.4 us (97%)
  local copies, waits for them, and re-layouts  2.29 us (2%)
    pallas_call x1, Pallas kernels, shards(): pl.pallas_call(kernel, name='parity_attention', out_shape=jax.ShapeDtypeS...  97.4 us
    reshape x1, local copies, waits for them, and re-layouts, shards(): return out.reshape(4 * PIECE, TOK).T  2.29 us

profile of v2, /device:TPU:37, one launch (start us, length us, event | category | flops | bytes accessed | tf_op | source)
XLA Modules:
  0.0 99.6 jit_solution(13378051418344323336)
XLA Ops:
  0.0 97.4 %parity_attention.1 = bf16[4,192,512]{2,1,0:T(8,128)(2,1)} custom-call(bf16[512,1024]{1,0:T(8,128)(2,1)} %q_hbm.1, bf16[512,1024]{1,0:T(8,128)(2,1)} %k_hbm.1, bf16[512,1024]{1,0:T(8,128)(2,1)} %v_hbm.1, bf16[192,1024]{1,0:T(8,128)(2,1)} %bitcast.6, f32[8,512]{1,0:T(8,128)} %bitcast.7, f32[8,128]{1,0:T(8,128)} %bitcast.8), custom_call_target="tpu_custom_call" | custom-call | flops 8000000000 | bytes 5242880 | tf_op jit(solution)/shard_map/parity_attention/pallas_call | solution.py:471
  97.4 2.3 %copy.7 = bf16[768,512]{0,1:T(8,128)(2,1)} copy(bf16[768,512]{1,0:T(8,128)(2,1)} %bitcast.5) | data formatting | bytes 1572864 | tf_op jit(solution)/shard_map/reshape | solution.py:526

commit v3 on v2

--- a/solution.py
+++ b/solution.py
@@ -35,7 +35,8 @@
     return jnp.dot(a, b, preferred_element_type=F32)
 
 
-EARLY = {0: (0, 2), 7: (1, 3)}
+EARLY = {7: (1, 3)}
+LAGS = (3, 9, 20)
 
 
 def fold(i):
@@ -95,6 +96,78 @@
         top = val.astype(BF).astype(F32)
         return jnp.concatenate([top, val - top], axis=0).astype(BF)
 
+    loads[0].wait()
+    pl.semaphore_wait(bar, len(peers))
+
+    def cut(b):
+        return pl.ds(b * CUT, CUT)
+
+    def chunk(b):
+        return pl.ds(b * CHUNK, CHUNK)
+
+    def kq(q):
+        turn = 1 + 2 * lax.rem(k0, 2)
+        return lax.rem(k0 + (0, turn, 4 - turn, 2)[q], 4)
+
+    def wz(b, i):
+        if i < 2:
+            ref = wb.at[y, k0, chunk(b)]
+            dz = 2 if i == 0 else -2
+        else:
+            ref = wb.at[y, lax.rem(k0 + (3 if b < 2 else 1), 4), chunk(b)]
+            dz = 2 if b < 2 else -2
+        return remote(ref, ref, wz_s.at[b, i], wz_r.at[b, i], at(0, dz))
+
+    def wz_wait(b, i):
+        ref = wb.at[y, lax.rem(k0 + (3, 1, 2)[i], 4), chunk(b)]
+        remote(ref, ref, wz_s.at[b, i], wz_r.at[b, i], at(0, 0)).wait_recv()
+
+    def wy(q, b, i):
+        if i < 2:
+            ref = wb.at[y, kq(q), chunk(b)]
+            dy = 1 if i == 0 else -1
+        else:
+            ref = wb.at[lax.rem(y + (3 if b < 2 else 1), NY), kq(q), chunk(b)]
+            dy = 1 if b < 2 else -1
+        return remote(ref, ref, wy_s.at[q, b, i], wy_r.at[q, b, i], at(dy, 0))
+
+    def wy_wait(q, b, i):
+        ref = wb.at[lax.rem(y + (3, 1, 2)[i], NY), kq(q), chunk(b)]
+        remote(ref, ref, wy_s.at[q, b, i], wy_r.at[q, b, i], at(0, 0)).wait_recv()
+
+    def y_send(q, b):
+        wy(q, b, 0).start()
+        wy(q, b, 1).start()
+
+    def y_forward(q, b):
+        wy_wait(q, b, b // 2)
+        wy(q, b, 2).start()
+        wy_wait(q, b, 1 - b // 2)
+
+    def turn(q, bs):
+        for b in bs:
+            y_forward(q, b)
+            if q < 3:
+                if q == 2:
+                    wz_wait(b, 2)
+                y_send(q + 1, b)
+
+    def y_last(q):
+        for b in CHUNKS:
+            wy_wait(q, b, 2)
+
+    def z_forward(b):
+        wz_wait(b, b // 2)
+        wz(b, 2).start()
+        wz_wait(b, 1 - b // 2)
+        y_send(1, b)
+
+    for b in CHUNKS:
+        y_send(0, b)
+    for b in (0, 2):
+        wz(b, 0).start()
+        wz(b, 1).start()
+
     loads[1].wait()
     loads[2].wait()
     tail = two_terms(cum[:, TOK - 1:TOK] + jnp.zeros((HEADS, HD), F32))
@@ -104,9 +177,6 @@
         keys = (kb[:, i * HD:(i + 1) * HD].astype(F32) * jnp.exp(last - col)).astype(BF)
         ust[i, 0:HD] = tn(keys, vb[:, i * HD:(i + 1) * HD]).astype(BF)
         ust[i, HD:SLOT] = tail
-    loads[0].wait()
-    pl.semaphore_wait(bar, len(peers))
-
     def send_z(src, dst, i):
         def one(o, _):
             to = lax.rem(z + o, NZ)
@@ -120,72 +190,6 @@
         return remote(src.at[some], dst.at[some], st_s.at[i], st_r.at[i], at(0, 0))
 
     send_z(ust, urecv, 0)
-
-    def cut(b):
-        return pl.ds(b * CUT, CUT)
-
-    def chunk(b):
-        return pl.ds(b * CHUNK, CHUNK)
-
-    def kq(q):
-        turn = 1 + 2 * lax.rem(k0, 2)
-        return lax.rem(k0 + (0, turn, 4 - turn, 2)[q], 4)
-
-    def wz(b, i):
-        if i < 2:
-            ref = wb.at[y, k0, chunk(b)]
-            dz = 2 if i == 0 else -2
-        else:
-            ref = wb.at[y, lax.rem(k0 + (3 if b < 2 else 1), 4), chunk(b)]
-            dz = 2 if b < 2 else -2
-        return remote(ref, ref, wz_s.at[b, i], wz_r.at[b, i], at(0, dz))
-
-    def wz_wait(b, i):
-        ref = wb.at[y, lax.rem(k0 + (3, 1, 2)[i], 4), chunk(b)]
-        remote(ref, ref, wz_s.at[b, i], wz_r.at[b, i], at(0, 0)).wait_recv()
-
-    def wy(q, b, i):
-        if i < 2:
-            ref = wb.at[y, kq(q), chunk(b)]
-            dy = 1 if i == 0 else -1
-        else:
-            ref = wb.at[lax.rem(y + (3 if b < 2 else 1), NY), kq(q), chunk(b)]
-            dy = 1 if b < 2 else -1
-        return remote(ref, ref, wy_s.at[q, b, i], wy_r.at[q, b, i], at(dy, 0))
-
-    def wy_wait(q, b, i):
-        ref = wb.at[lax.rem(y + (3, 1, 2)[i], NY), kq(q), chunk(b)]
-        remote(ref, ref, wy_s.at[q, b, i], wy_r.at[q, b, i], at(0, 0)).wait_recv()
-
-    def y_send(q, b):
-        wy(q, b, 0).start()
-        wy(q, b, 1).start()
-
-    def y_forward(q, b):
-        wy_wait(q, b, b // 2)
-        wy(q, b, 2).start()
-        wy_wait(q, b, 1 - b // 2)
-
-    def turn(q, bs):
-        for b in bs:
-            y_forward(q, b)
-            if q < 3:
-                if q == 2:
-                    wz_wait(b, 2)
-                y_send(q + 1, b)
-
-    def y_last(q):
-        for b in CHUNKS:
-            wy_wait(q, b, 2)
-
-    def z_forward(b):
-        wz_wait(b, b // 2)
-        wz(b, 2).start()
-        wz_wait(b, 1 - b // 2)
-        y_send(1, b)
-
-    for b in CHUNKS:
-        y_send(0, b)
 
     loads[3].wait()
     causal = lax.broadcasted_iota(jnp.int32, (HALF, HALF), 0) >= lax.broadcasted_iota(jnp.int32, (HALF, HALF), 1)
@@ -301,7 +305,7 @@
 
         @pl.when(mine)
         def _():
-            fbuf[n % 4, 0:m] = res
+            fbuf[n % 8, 0:m] = res
 
         @pl.when(jnp.logical_not(mine))
         def _():
@@ -315,7 +319,7 @@
         @pl.when(mine)
         def _():
             mate_copy(n, unit).wait_recv()
-            val = (fbuf[n % 4, 0:m] + dbuf[yy, half, ks].astype(F32)).astype(BF)
+            val = (fbuf[n % 8, 0:m] + dbuf[yy, half, ks].astype(F32)).astype(BF)
 
             @pl.when(far == 0)
             def _():
@@ -416,7 +420,7 @@
     hook(lambda: y_last(3))
     add((3,), (3,), (1, 0))
 
-    stages = ((0, compute), (3, pair), (9, passed), (20, total))
+    stages = ((0, compute), (LAGS[0], pair), (LAGS[1], passed), (LAGS[2], total))
     for n in range(len(order) + stages[-1][0]):
         for fn in hooks.get(n, ()):
             fn()
@@ -424,11 +428,15 @@
             if 0 <= n - lag < len(order):
                 fn(n - lag, order[n - lag])
 
+    def out_copy(i):
+        return pltpu.make_async_copy(otb.at[i], out_hbm.at[i], out_sem.at[i])
+
+    for kk in range(2):
+        out_copy(2 * kk + h).start()
     for kk in range(2):
         for i in range(2):
             back_wait(kk, i)
-    final = pltpu.make_async_copy(otb, out_hbm, out_sem.at[0])
-    final.start()
+        out_copy(2 * kk + 1 - h).start()
 
     for b in CHUNKS:
         for i in range(3):
@@ -460,7 +468,8 @@
                 back(one, 0).wait_send()
                 back(one, 1).wait_send()
 
-    final.wait()
+    for i in range(4):
+        out_copy(i).wait()
 
 
 def shards(query_rows, key_rows, value_rows, log_decay, norm_gain, out_proj):
@@ -492,14 +501,14 @@
             vmem((NZ, HD, HD), BF),
             vmem((NZ, HD, HD), BF),
             vmem((NY, 2, 4, PIECE, TOK), BF),
-            vmem((4, 2, PIECE, TOK), F32),
+            vmem((8, 2, PIECE, TOK), F32),
             vmem((2, NY, 4, CUT, TOK), BF),
             vmem((2, 2, PIECE, TOK), BF),
             vmem((2, 2, 2, PIECE, TOK), BF),
             vmem((2, PIECE, TOK), BF),
             vmem((4, PIECE, TOK), BF),
             dma((4,)),
-            dma((1,)),
+            dma((4,)),
             dma((4, 3)),
             dma((4, 3)),
             dma((4, 4, 3)),

time: 99.9 us -> 97.6 us (0.977)
  the two profiles are of different devices: /device:TPU:37 before, /device:TPU:16 now
where the time goes in v3:
time: 97.6 us; the launch traced here: 96.1 us
  Pallas kernels  93.8 us (96%)
  local copies, waits for them, and re-layouts  2.29 us (2%)
    pallas_call x1, Pallas kernels, shards(): pl.pallas_call(kernel, name='parity_attention', out_shape=jax.ShapeDtypeS...  93.8 us
    reshape x1, local copies, waits for them, and re-layouts, shards(): return out.reshape(4 * PIECE, TOK).T  2.29 us

profile of v3, /device:TPU:16, one launch (start us, length us, event | category | flops | bytes accessed | tf_op | source)
XLA Modules:
  0.0 96.1 jit_solution(1185187335351739630)
XLA Ops:
  0.0 93.8 %parity_attention.1 = bf16[4,192,512]{2,1,0:T(8,128)(2,1)} custom-call(bf16[512,1024]{1,0:T(8,128)(2,1)} %q_hbm.1, bf16[512,1024]{1,0:T(8,128)(2,1)} %k_hbm.1, bf16[512,1024]{1,0:T(8,128)(2,1)} %v_hbm.1, bf16[192,1024]{1,0:T(8,128)(2,1)} %bitcast.6, f32[8,512]{1,0:T(8,128)} %bitcast.7, f32[8,128]{1,0:T(8,128)} %bitcast.8), custom_call_target="tpu_custom_call" | custom-call | flops 8000000000 | bytes 5242880 | tf_op jit(solution)/shard_map/parity_attention/pallas_call | solution.py:480
  93.8 2.3 %copy.7 = bf16[768,512]{0,1:T(8,128)(2,1)} copy(bf16[768,512]{1,0:T(8,128)(2,1)} %bitcast.5) | data formatting | bytes 1572864 | tf_op jit(solution)/shard_map/reshape | solution.py:535

commit v4 on v3

--- a/solution.py
+++ b/solution.py
@@ -36,7 +36,7 @@
 
 
 EARLY = {7: (1, 3)}
-LAGS = (3, 9, 20)
+LAGS = (2, 7, 14)
 
 
 def fold(i):
@@ -80,6 +80,78 @@
     for dev in peers:
         pl.semaphore_signal(bar, inc=1, device_id=dev, device_id_type=MESH)
 
+    loads[0].wait()
+    pl.semaphore_wait(bar, len(peers))
+
+    def cut(b):
+        return pl.ds(b * CUT, CUT)
+
+    def chunk(b):
+        return pl.ds(b * CHUNK, CHUNK)
+
+    def kq(q):
+        turn = 1 + 2 * lax.rem(k0, 2)
+        return lax.rem(k0 + (0, turn, 4 - turn, 2)[q], 4)
+
+    def wz(b, i):
+        if i < 2:
+            ref = wb.at[y, k0, chunk(b)]
+            dz = 2 if i == 0 else -2
+        else:
+            ref = wb.at[y, lax.rem(k0 + (3 if b < 2 else 1), 4), chunk(b)]
+            dz = 2 if b < 2 else -2
+        return remote(ref, ref, wz_s.at[b, i], wz_r.at[b, i], at(0, dz))
+
+    def wz_wait(b, i):
+        ref = wb.at[y, lax.rem(k0 + (3, 1, 2)[i], 4), chunk(b)]
+        remote(ref, ref, wz_s.at[b, i], wz_r.at[b, i], at(0, 0)).wait_recv()
+
+    def wy(q, b, i):
+        if i < 2:
+            ref = wb.at[y, kq(q), chunk(b)]
+            dy = 1 if i == 0 else -1
+        else:
+            ref = wb.at[lax.rem(y + (3 if b < 2 else 1), NY), kq(q), chunk(b)]
+            dy = 1 if b < 2 else -1
+        return remote(ref, ref, wy_s.at[q, b, i], wy_r.at[q, b, i], at(dy, 0))
+
+    def wy_wait(q, b, i):
+        ref = wb.at[lax.rem(y + (3, 1, 2)[i], NY), kq(q), chunk(b)]
+        remote(ref, ref, wy_s.at[q, b, i], wy_r.at[q, b, i], at(0, 0)).wait_recv()
+
+    def y_send(q, b):
+        wy(q, b, 0).start()
+        wy(q, b, 1).start()
+
+    def y_forward(q, b):
+        wy_wait(q, b, b // 2)
+        wy(q, b, 2).start()
+        wy_wait(q, b, 1 - b // 2)
+
+    def turn(q, bs):
+        for b in bs:
+            y_forward(q, b)
+            if q < 3:
+                if q == 2:
+                    wz_wait(b, 2)
+                y_send(q + 1, b)
+
+    def y_last(q):
+        for b in CHUNKS:
+            wy_wait(q, b, 2)
+
+    def z_forward(b):
+        wz_wait(b, b // 2)
+        wz(b, 2).start()
+        wz_wait(b, 1 - b // 2)
+        y_send(1, b)
+
+    for b in CHUNKS:
+        y_send(0, b)
+    for b in (0, 2):
+        wz(b, 0).start()
+        wz(b, 1).start()
+
     d = decay_ref[...]
     hi = d.astype(BF).astype(F32)
     mid = (d - hi).astype(BF).astype(F32)
@@ -95,78 +167,6 @@
     def two_terms(val):
         top = val.astype(BF).astype(F32)
         return jnp.concatenate([top, val - top], axis=0).astype(BF)
-
-    loads[0].wait()
-    pl.semaphore_wait(bar, len(peers))
-
-    def cut(b):
-        return pl.ds(b * CUT, CUT)
-
-    def chunk(b):
-        return pl.ds(b * CHUNK, CHUNK)
-
-    def kq(q):
-        turn = 1 + 2 * lax.rem(k0, 2)
-        return lax.rem(k0 + (0, turn, 4 - turn, 2)[q], 4)
-
-    def wz(b, i):
-        if i < 2:
-            ref = wb.at[y, k0, chunk(b)]
-            dz = 2 if i == 0 else -2
-        else:
-            ref = wb.at[y, lax.rem(k0 + (3 if b < 2 else 1), 4), chunk(b)]
-            dz = 2 if b < 2 else -2
-        return remote(ref, ref, wz_s.at[b, i], wz_r.at[b, i], at(0, dz))
-
-    def wz_wait(b, i):
-        ref = wb.at[y, lax.rem(k0 + (3, 1, 2)[i], 4), chunk(b)]
-        remote(ref, ref, wz_s.at[b, i], wz_r.at[b, i], at(0, 0)).wait_recv()
-
-    def wy(q, b, i):
-        if i < 2:
-            ref = wb.at[y, kq(q), chunk(b)]
-            dy = 1 if i == 0 else -1
-        else:
-            ref = wb.at[lax.rem(y + (3 if b < 2 else 1), NY), kq(q), chunk(b)]
-            dy = 1 if b < 2 else -1
-        return remote(ref, ref, wy_s.at[q, b, i], wy_r.at[q, b, i], at(dy, 0))
-
-    def wy_wait(q, b, i):
-        ref = wb.at[lax.rem(y + (3, 1, 2)[i], NY), kq(q), chunk(b)]
-        remote(ref, ref, wy_s.at[q, b, i], wy_r.at[q, b, i], at(0, 0)).wait_recv()
-
-    def y_send(q, b):
-        wy(q, b, 0).start()
-        wy(q, b, 1).start()
-
-    def y_forward(q, b):
-        wy_wait(q, b, b // 2)
-        wy(q, b, 2).start()
-        wy_wait(q, b, 1 - b // 2)
-
-    def turn(q, bs):
-        for b in bs:
-            y_forward(q, b)
-            if q < 3:
-                if q == 2:
-                    wz_wait(b, 2)
-                y_send(q + 1, b)
-
-    def y_last(q):
-        for b in CHUNKS:
-            wy_wait(q, b, 2)
-
-    def z_forward(b):
-        wz_wait(b, b // 2)
-        wz(b, 2).start()
-        wz_wait(b, 1 - b // 2)
-        y_send(1, b)
-
-    for b in CHUNKS:
-        y_send(0, b)
-    for b in (0, 2):
-        wz(b, 0).start()
-        wz(b, 1).start()
 
     loads[1].wait()
     loads[2].wait()

time: 97.6 us -> 97.4 us (level); the launches traced: 96.1 us -> 97.2 us
  Pallas kernels: 93.8 us -> 94.9 us
    pallas_call x1, Pallas kernels: 93.8 us -> 94.9 us  [shards(): pl.pallas_call(kernel, name='parity_attention', out_shape=jax.ShapeDtypeS...]
where the time goes in v4:
time: 97.4 us; the launch traced here: 97.2 us
  Pallas kernels  94.9 us (97%)
  local copies, waits for them, and re-layouts  2.29 us (2%)
    pallas_call x1, Pallas kernels, shards(): pl.pallas_call(kernel, name='parity_attention', out_shape=jax.ShapeDtypeS...  94.9 us
    reshape x1, local copies, waits for them, and re-layouts, shards(): return out.reshape(4 * PIECE, TOK).T  2.29 us

profile of v4, /device:TPU:16, one launch (start us, length us, event | category | flops | bytes accessed | tf_op | source)
XLA Modules:
  0.0 97.2 jit_solution(12188493289233923635)
XLA Ops:
  0.0 94.9 %parity_attention.1 = bf16[4,192,512]{2,1,0:T(8,128)(2,1)} custom-call(bf16[512,1024]{1,0:T(8,128)(2,1)} %q_hbm.1, bf16[512,1024]{1,0:T(8,128)(2,1)} %k_hbm.1, bf16[512,1024]{1,0:T(8,128)(2,1)} %v_hbm.1, bf16[192,1024]{1,0:T(8,128)(2,1)} %bitcast.6, f32[8,512]{1,0:T(8,128)} %bitcast.7, f32[8,128]{1,0:T(8,128)} %bitcast.8), custom_call_target="tpu_custom_call" | custom-call | flops 8000000000 | bytes 5242880 | tf_op jit(solution)/shard_map/parity_attention/pallas_call | solution.py:480
  94.9 2.3 %copy.7 = bf16[768,512]{0,1:T(8,128)(2,1)} copy(bf16[768,512]{1,0:T(8,128)(2,1)} %bitcast.5) | data formatting | bytes 1572864 | tf_op jit(solution)/shard_map/reshape | solution.py:535
